TPU v7x, 128 devices: a whole 4x4x4 slice. The times are simulated.
128 devices in a mesh: dp: 4 (over z), seq: 32 (over y, x, core).
Axes of the slice: x: 4, y: 4, z: 4, core: 2. Of those that a mesh axis runs over, the one named last changes fastest.
Arguments:
- queries: bfloat16 [16384, 4096], P(('dp', 'seq')), parts along dimension 0, may hold values from -7 to 7
- key_vectors: bfloat16 [16384, 512], P(('dp', 'seq')), parts along dimension 0, may hold values from -6 to 6
- value_vectors: bfloat16 [16384, 512], P(('dp', 'seq')), parts along dimension 0, may hold values from -12 to 12
- residual: bfloat16 [16384, 2048], P(('dp', 'seq')), parts along dimension 0, may hold values from -16 to 16
- out_weight: bfloat16 [4096, 2048], P('seq'), may hold values from -0.09375 to 0.09375
- norm_gain: float32 [2048], replicated, may hold values from 0.1 to 1.9
- routes: int32 [16384, 8], P(('dp', 'seq')), parts along dimension 0, may hold values from 0 to 63, all different within a row; in each aligned block of 128 rows (0 to 127, 128 to 255, ...) at most 24 rows name the same one
- route_gates: float32 [16384, 8], P(('dp', 'seq')), parts along dimension 0, may hold values from 0.05 to 1
- w_gate: bfloat16 [64, 2048, 768], P('seq'), may hold values from -0.125 to 0.125
- w_up: bfloat16 [64, 2048, 768], P('seq'), may hold values from -0.125 to 0.125
- w_down: bfloat16 [64, 768, 2048], P('seq'), may hold values from -0.21875 to 0.21875
Outputs:
- stream: bfloat16 [16384, 2048], P(('dp', 'seq')), parts along dimension 0
- layer_out: bfloat16 [16384, 2048], P(('dp', 'seq')), parts along dimension 0
There are 4 independent parts, one for each index of `dp`. A program takes and returns all parts, laid end to end along the dimension named above; an argument that names none is the same for every part. Nothing has to cross between parts.
Inputs may be any that keep to these rules, and one draw needn't show every extreme that they name: `routes`: each token names 8 different experts; among the 128 tokens of one device no expert is named more than 24 times.
All inputs are finite; a program needn't handle non-finite values.
Results may differ from a plain program's by a relative error of at most 0.019.
Values may be sent and summed in bfloat16 or wider, within the bound.
No kernel may reach another device: no remote copies, remote signals or barrier semaphores. Data moves between devices by JAX's collectives and lax.ppermute only.
A program may use at most 128 MiB of HBM per device.

v0:
```python
import jax
import jax.numpy as jnp
from jax import lax
from jax.sharding import PartitionSpec as P

HEADS = 32
KV_HEADS = 4
HEAD_DIM = 128
TOPK = 8


def attend_block(block_queries, first_row, all_keys, all_values):
    score_scale = HEAD_DIM ** (-0.5)
    scores = (
        jnp.einsum("qhd,khd->hqk", block_queries, all_keys, preferred_element_type=jnp.float32)
        * score_scale
    )
    shape_pair = (block_queries.shape[0], all_keys.shape[0])
    query_pos = first_row + lax.broadcasted_iota(jnp.int32, shape_pair, 0)
    key_pos = lax.broadcasted_iota(jnp.int32, shape_pair, 1)
    scores = jnp.where((key_pos <= query_pos)[None, :, :], scores, -1e30)
    row_max = jnp.max(scores, axis=2, keepdims=True)
    weight = jnp.exp(scores - row_max)
    probs = (weight / jnp.sum(weight, axis=2, keepdims=True)).astype(jnp.bfloat16)
    return jnp.einsum("hqk,khd->qhd", probs, all_values, preferred_element_type=jnp.float32).astype(
        jnp.bfloat16
    )


def spread_heads(queries, key_vectors, value_vectors):
    local_tokens = queries.shape[0]
    copies = HEADS // KV_HEADS
    key_send = jnp.repeat(
        key_vectors.reshape(local_tokens, KV_HEADS, HEAD_DIM), copies, axis=1
    ).reshape(local_tokens, -1)
    value_send = jnp.repeat(
        value_vectors.reshape(local_tokens, KV_HEADS, HEAD_DIM), copies, axis=1
    ).reshape(local_tokens, -1)
    return (key_send, value_send)


def heads_attend(heads_q, heads_k, heads_v):
    all_tokens = heads_q.shape[0]
    heads_here = heads_q.shape[1] // HEAD_DIM
    heads_q = heads_q.reshape(all_tokens, heads_here, HEAD_DIM)
    heads_k = heads_k.reshape(all_tokens, heads_here, HEAD_DIM)
    heads_v = heads_v.reshape(all_tokens, heads_here, HEAD_DIM)
    block_rows = min(all_tokens, max(512, all_tokens // 16))
    block_count = all_tokens // block_rows
    pieces_out = []
    for block in range(block_count):
        begin = block * block_rows
        finish = begin + block_rows
        pieces_out.append(
            attend_block(heads_q[begin:finish], begin, heads_k[:finish], heads_v[:finish])
        )
    return jnp.concatenate(pieces_out, axis=0).reshape(all_tokens, heads_here * HEAD_DIM)


def body(
    queries,
    key_vectors,
    value_vectors,
    residual,
    out_weight,
    norm_gain,
    routes,
    route_gates,
    w_gate,
    w_up,
    w_down,
):
    local_tokens = queries.shape[0]
    width = residual.shape[1]
    devices_seq = lax.axis_size("seq")
    key_send, value_send = spread_heads(queries, key_vectors, value_vectors)
    heads_q, heads_k, heads_v = (
        lax.all_to_all(queries, "seq", split_axis=1, concat_axis=0, tiled=True),
        lax.all_to_all(key_send, "seq", split_axis=1, concat_axis=0, tiled=True),
        lax.all_to_all(value_send, "seq", split_axis=1, concat_axis=0, tiled=True),
    )
    attended = heads_attend(heads_q, heads_k, heads_v)
    attn_sum = lax.psum_scatter(
        jnp.dot(attended, out_weight, preferred_element_type=jnp.float32).astype(jnp.bfloat16),
        "seq",
        scatter_dimension=0,
        tiled=True,
    ).astype(jnp.float32)
    stream = (residual.astype(jnp.float32) + attn_sum).astype(jnp.bfloat16)
    stream_f = stream.astype(jnp.float32)
    normed = (
        stream_f
        * lax.rsqrt(jnp.mean(stream_f * stream_f, axis=1, keepdims=True) + 1e-06)
        * norm_gain
    ).astype(jnp.bfloat16)
    route_share = route_gates / jnp.sum(route_gates, axis=1, keepdims=True)
    experts_here = w_gate.shape[0]
    experts_all = experts_here * devices_seq
    capacity = 3 * local_tokens * TOPK // (2 * experts_all)
    flat_routes = routes.reshape(-1)
    expert_hits = (
        flat_routes[:, None] == jnp.arange(experts_all, dtype=jnp.int32)[None, :]
    ).astype(jnp.int32)
    slot_rank = jnp.sum((jnp.cumsum(expert_hits, axis=0) - 1) * expert_hits, axis=1)
    slot_index = flat_routes * capacity + slot_rank
    send_rows = (
        jnp.zeros((experts_all * capacity, width), jnp.bfloat16)
        .at[slot_index]
        .set(jnp.repeat(normed, TOPK, axis=0))
    )
    send_rows = send_rows.reshape(devices_seq, experts_here, capacity, width)
    arrived = lax.all_to_all(send_rows, "seq", split_axis=0, concat_axis=0, tiled=True)
    gate_part = jnp.einsum("secd,edf->secf", arrived, w_gate, preferred_element_type=jnp.float32)
    up_part = jnp.einsum("secd,edf->secf", arrived, w_up, preferred_element_type=jnp.float32)
    hidden = (jax.nn.silu(gate_part) * up_part).astype(jnp.bfloat16)
    expert_out = jnp.einsum(
        "secf,efd->secd", hidden, w_down, preferred_element_type=jnp.float32
    ).astype(jnp.bfloat16)
    returned = lax.all_to_all(expert_out, "seq", split_axis=0, concat_axis=0, tiled=True)
    routed = returned.reshape(-1, width)[slot_index].reshape(local_tokens, TOPK, width)
    expert_sum = jnp.einsum("trd,tr->td", routed.astype(jnp.float32), route_share)
    layer_out = (stream_f + expert_sum).astype(jnp.bfloat16)
    return (stream, layer_out)


def solution(mesh):
    in_specs = (
        P(("dp", "seq"), None),
        P(("dp", "seq"), None),
        P(("dp", "seq"), None),
        P(("dp", "seq"), None),
        P("seq", None),
        P(),
        P(("dp", "seq"), None),
        P(("dp", "seq"), None),
        P("seq", None, None),
        P("seq", None, None),
        P("seq", None, None),
    )
    out_specs = (P(("dp", "seq"), None), P(("dp", "seq"), None))
    return jax.shard_map(body, mesh=mesh, in_specs=in_specs, out_specs=out_specs, check_vma=False)
```

profile of v0, /device:TPU:0, one launch (start us, length us, event | category | flops | bytes accessed | tf_op | source)
XLA Modules:
  0.0 474.9 jit_solution(17005781733392410582)
XLA Ops:
  9.4 7.4 %all-to-all-start.1 = ((bf16[128,32,128]{2,0,1:T(8,128)(2,1)}), bf16[128,32,128]{2,0,1:T(8,128)(2,1)S(1)}, u32[]{:S(2)}, u32[]{:S(2)}) async-start(bf16[128,32,128]{2,0,1:T(8,128)(2,1)} %bitcast.3), calls=%async_computation.1 | async-start | bytes 2097152 | tf_op jit(solution)/shard_map/all_to_all | solution.py:79
  17.7 16.4 %all-to-all-done.1 = bf16[128,32,128]{2,0,1:T(8,128)(2,1)S(1)} async-done(((bf16[128,32,128]{2,0,1:T(8,128)(2,1)}), bf16[128,32,128]{2,0,1:T(8,128)(2,1)S(1)}, u32[]{:S(2)}, u32[]{:S(2)}) %all-to-all-start.1) | async-done | bytes 1048608 | tf_op jit(solution)/shard_map/all_to_all | solution.py:79
  35.3 3.9 all-to-all-start.2
  39.3 2.3 copy.40
  41.5 15.1 %all-to-all-done.2 = bf16[128,32,128]{2,0,1:T(8,128)(2,1)S(1)} async-done(((bf16[128,32,128]{2,0,1:T(8,128)(2,1)}), bf16[128,32,128]{2,0,1:T(8,128)(2,1)S(1)}, u32[]{:S(2)}, u32[]{:S(2)}) %all-to-all-start.2) | async-done | bytes 1048608 | tf_op jit(solution)/shard_map/all_to_all | solution.py:80
  56.6 4.7 all-to-all-start
  74.4 4.2 all-to-all-done
  78.6 2.3 fusion.71
  80.9 1.7 copy.41
  84.2 1.7 copy.45
  85.8 1.7 copy.46
  87.5 1.6 copy.47
  89.1 1.7 copy.48
  92.5 1.7 copy.50
  95.7 1.9 fusion.44
  109.3 2.2 fusion.78
  112.7 2.0 fusion.79
  116.1 2.3 fusion.48
  125.8 2.2 fusion.50
  128.1 8.2 %convolution_convert_fusion = bf16[4096,2048]{1,0:T(8,128)(2,1)} fusion(bf16[128,2048]{1,0:T(8,128)(2,1)S(1)} %copy-done, bf16[4096,1,128]{2,0,1:T(8,128)(2,1)S(1)} %fusion.50), kind=kOutput, calls=%fused_computation.2 | convolution fusion | flops 2155872256 | bytes 18350080 | tf_op jit(solution)/shard_map/dot_general | solution.py:84
  137.3 18.0 %reduce-window.6 = s32[64,8,128]{2,1,0:T(8,128)S(1)} reduce-window(s32[64,8,128]{2,1,0:T(8,128)S(1)} %fusion.69, s32[]{:T(128)} %constant.9.clone.1), window={size=1x1x128 pad=0_0x0_0x127_0}, to_apply=%region_17.18 | reduce-window | flops 8323072 | bytes 524292 | tf_op jit(solution)/shard_map/reduce-window
  156.2 94.1 %reduce-scatter.2.cloned.1.call-done = bf16[128,2048]{1,0:T(8,128)(2,1)} async-done(((bf16[4096,2048]{1,0:T(8,128)(2,1)}), bf16[128,2048]{1,0:T(8,128)(2,1)}) %reduce-scatter.2.cloned.1.call-update) | async-done | bytes 524304 | tf_op jit(solution)/shard_map/reduce_scatter | solution.py:83
  251.8 10.2 %scatter_custom_fusion = bf16[1536,2048]{1,0:T(8,128)(2,1)} fusion(s32[1024]{0:T(1024)S(1)} %bitcast.245, bf16[]{:T(256)} %constant.7.clone.1, bf16[128,2048]{1,0:T(8,128)(2,1)S(1)} %fusion.61), kind=kCustom, calls=%fused_computation.41 | custom fusion | bytes 6815746 | tf_op jit(solution)/shard_map/scatter | solution.py:109
  262.0 79.2 %all_to_all.58 = bf16[32,2,24,2048]{3,2,1,0:T(8,128)(2,1)S(1)} all-to-all(bf16[32,2,24,2048]{3,2,1,0:T(8,128)(2,1)} %bitcast.201), channel_id=1, replica_groups=mesh['dp'=4,'seq'=32] {'seq'}, dimensions={0} | all-to-all | bytes 12582912 | tf_op jit(solution)/shard_map/all_to_all | solution.py:112
  341.2 7.5 %fusion.4 = f32[2,32,24,768]{3,2,1,0:T(8,128)S(1)} fusion(bf16[2,2048,768]{2,1,0:T(8,128)(2,1)} %param.20, bf16[32,2,24,2048]{3,2,1,0:T(8,128)(2,1)S(1)} %all_to_all.58), kind=kOutput, calls=%fused_computation.15 | convolution fusion | flops 4831838208 | bytes 17301504 | tf_op jit(solution)/shard_map/secd,edf->secf/dot_general | solution.py:114
  348.7 6.9 %fusion.6 = f32[2,32,24,768]{3,2,1,0:T(8,128)} fusion(bf16[2,2048,768]{2,1,0:T(8,128)(2,1)S(1)} %bitcast.248, bf16[32,2,24,2048]{3,2,1,0:T(8,128)(2,1)S(1)} %all_to_all.58), kind=kOutput, calls=%fused_computation.17 | convolution fusion | flops 4831838208 | bytes 17301504 | tf_op jit(solution)/shard_map/secd,edf->secf/dot_general | solution.py:113
  355.6 9.0 %convert_bitcast_fusion = bf16[32,2,24,2048]{3,2,0,1:T(8,128)(2,1)S(1)} fusion(bf16[2,768,2048]{2,1,0:T(8,128)(2,1)} %param.21, f32[2,32,24,768]{3,2,1,0:T(8,128)S(1)} %fusion.4, f32[2,32,24,768]{3,2,1,0:T(8,128)} %fusion.6), kind=kOutput, calls=%fused_computation.19 | convolution fusion | flops 4842061824 | bytes 22020096 | tf_op jit(solution)/shard_map/secf,efd->secd/dot_general | solution.py:116
  364.7 3.2 copy.58
  367.9 5.0 %all-to-all-start.4 = ((bf16[32,2,24,2048]{3,2,1,0:T(8,128)(2,1)}), bf16[32,2,24,2048]{3,2,1,0:T(8,128)(2,1)}, u32[]{:S(2)}, u32[]{:S(2)}) async-start(bf16[32,2,24,2048]{3,2,1,0:T(8,128)(2,1)} %copy.58), calls=%async_computation.5 | async-start | bytes 12582912 | tf_op jit(solution)/shard_map/all_to_all | solution.py:119
  373.1 77.7 %all-to-all-done.4 = bf16[32,2,24,2048]{3,2,1,0:T(8,128)(2,1)} async-done(((bf16[32,2,24,2048]{3,2,1,0:T(8,128)(2,1)}), bf16[32,2,24,2048]{3,2,1,0:T(8,128)(2,1)}, u32[]{:S(2)}, u32[]{:S(2)}) %all-to-all-start.4) | async-done | bytes 6291488 | tf_op jit(solution)/shard_map/all_to_all | solution.py:119
  450.8 12.4 %gather_fusion = bf16[1024,2048]{1,0:T(8,128)(2,1)} fusion(bf16[1536,2048]{1,0:T(8,128)(2,1)} %bitcast.70, s32[1024]{0:T(1024)S(1)} %broadcast_clamp_fusion), kind=kCustom, calls=%fused_computation | custom fusion | bytes 8392704 | tf_op jit(solution)/shard_map/gather | solution.py:120
  463.3 3.4 fusion.18
  (168 shorter events, 48.2 us)
Async XLA Ops:
  7.2 120.9 %copy-start = (bf16[128,2048]{1,0:T(8,128)(2,1)S(1)}, bf16[128,2048]{1,0:T(8,128)(2,1)}, u32[]{:S(2)}) copy-start(bf16[128,2048]{1,0:T(8,128)(2,1)} %param.15) | copy-start | bytes 1572868
  9.4 24.7 %all-to-all-start.1 = ((bf16[128,32,128]{2,0,1:T(8,128)(2,1)}), bf16[128,32,128]{2,0,1:T(8,128)(2,1)S(1)}, u32[]{:S(2)}, u32[]{:S(2)}) async-start(bf16[128,32,128]{2,0,1:T(8,128)(2,1)} %bitcast.3), calls=%async_computation.1 | async-start | bytes 2097152 | tf_op jit(solution)/shard_map/all_to_all | solution.py:79
  35.3 21.3 %all-to-all-start.2 = ((bf16[128,32,128]{2,0,1:T(8,128)(2,1)}), bf16[128,32,128]{2,0,1:T(8,128)(2,1)S(1)}, u32[]{:S(2)}, u32[]{:S(2)}) async-start(bf16[128,32,128]{2,0,1:T(8,128)(2,1)} %bitcast.219), calls=%async_computation.2 | async-start | bytes 2097152 | tf_op jit(solution)/shard_map/all_to_all | solution.py:80
  56.6 22.0 %all-to-all-start = ((bf16[128,32,128]{0,2,1:T(8,128)(2,1)}), bf16[128,32,128]{0,2,1:T(8,128)(2,1)}, u32[]{:S(2)}, u32[]{:S(2)}) async-start(bf16[128,32,128]{0,2,1:T(8,128)(2,1)} %bitcast.218), calls=%async_computation | async-start | bytes 2097152 | tf_op jit(solution)/shard_map/all_to_all | solution.py:78
  61.3 189.0 %reduce-scatter.2.cloned.1.call-start = ((), (), s32[]{:S(2)}) async-start(), calls=%async_computation.6 | async-start | bytes 17301504 | tf_op jit(solution)/shard_map/reduce_scatter | solution.py:83
  94.1 3.5 copy-start.20
  94.1 3.5 copy-start.27
  95.5 4.1 copy-start.18
  95.5 4.1 copy-start.26
  98.2 4.8 %copy-start.43 = (f32[512]{0:T(512)}, f32[512]{0:T(512)S(1)}, u32[]{:S(2)}) copy-start(f32[512]{0:T(512)S(1)} %get-tuple-element.14) | copy-start | bytes 6148
  98.2 3.8 copy-start.16
  98.2 3.8 copy-start.25
  100.9 2.8 copy-start.13
  100.9 2.8 copy-start.24
  100.9 2.8 copy-start.42
  103.8 2.6 copy-start.11
  103.8 2.6 copy-start.23
  103.8 2.6 copy-start.41
  105.0 2.8 copy-start.31
  107.7 3.8 copy-start.33
  111.5 3.1 copy-start.36
  116.0 2.5 copy-start.6
  116.0 2.6 copy-start.17
  118.6 2.3 copy-start.15
  136.3 114.0 %copy-start.14 = (bf16[128,2048]{1,0:T(8,128)(2,1)S(1)}, bf16[128,2048]{1,0:T(8,128)(2,1)}, u32[]{:S(2)}) copy-start(bf16[128,2048]{1,0:T(8,128)(2,1)} %param.14) | copy-start | bytes 1572868
  136.3 115.3 %copy-start.30 = (f32[2048]{0:T(1024)S(1)}, f32[2048]{0:T(1024)}, u32[]{:S(2)}) copy-start(f32[2048]{0:T(1024)} %param.16) | copy-start | bytes 24580
  251.6 215.1 %copy-start.2 = (bf16[128,2048]{1,0:T(8,128)(2,1)}, bf16[128,2048]{1,0:T(8,128)(2,1)S(1)}, u32[]{:S(2)}) copy-start(bf16[128,2048]{1,0:T(8,128)(2,1)S(1)} %get-tuple-element.3) | copy-start | bytes 1572868
  262.0 86.7 %slice-start = ((s8[6291456]{0:T(1024)(128)(4,1)}), s8[4194304]{0:T(1024)(128)(4,1)S(1)}, s32[]{:S(2)}) async-start(s8[6291456]{0:T(1024)(128)(4,1)} %bitcast.247), calls=%async_computation.7 | async-start | bytes 8388608
  341.2 7.5 %slice-start.1 = ((s8[6291456]{0:T(1024)(128)(4,1)}), s8[2097152]{0:T(1024)(128)(4,1)S(1)}, s32[]{:S(2)}) async-start(s8[6291456]{0:T(1024)(128)(4,1)} %bitcast.247), calls=%async_computation.8 | async-start | bytes 4194304
  367.9 5.0 %copy-start.29 = (f32[128,8]{0,1:T(8,128)S(1)}, f32[128,8]{0,1:T(8,128)}, u32[]{:S(2)}) copy-start(f32[128,8]{0,1:T(8,128)} %param.18) | copy-start | bytes 12292
  367.9 82.9 %all-to-all-start.4 = ((bf16[32,2,24,2048]{3,2,1,0:T(8,128)(2,1)}), bf16[32,2,24,2048]{3,2,1,0:T(8,128)(2,1)}, u32[]{:S(2)}, u32[]{:S(2)}) async-start(bf16[32,2,24,2048]{3,2,1,0:T(8,128)(2,1)} %copy.58), calls=%async_computation.5 | async-start | bytes 12582912 | tf_op jit(solution)/shard_map/all_to_all | solution.py:119
  450.8 17.0 %copy-start.1 = (bf16[128,2048]{1,0:T(8,128)(2,1)S(1)}, bf16[128,2048]{1,0:T(8,128)(2,1)}, u32[]{:S(2)}) copy-start(bf16[128,2048]{1,0:T(8,128)(2,1)} %param.15) | copy-start | bytes 1572868
  (21 other events, 27.9 us)
Sparse Core Ops, SparseCore 0:
  136.5 113.7 reduce-scatter.1
where the time goes:
time: 484 us; the launch traced here: 475 us
  waiting for transfers between devices  208 us (43%)
  blocking collectives  79.2 us (16%)
  local copies, waits for them, and re-layouts  64 us (13%)
  matrix products  57.3 us (12%)
  other arithmetic  31 us (6%)
  starting transfers between devices  21.1 us (4%)
  between operations  14.9 us (3%)
    reduce_scatter x1, waiting for transfers between devices, body(): lax.psum_scatter(jnp.dot(attended, out_weight, preferred_element_type=jnp...  94.1 us
    all_to_all x1, blocking collectives, body(): lax.all_to_all(send_rows, 'seq', split_axis=0, concat_axis=0, tiled=True)  79.2 us
    all_to_all x1, waiting for transfers between devices, body(): lax.all_to_all(expert_out, 'seq', split_axis=0, concat_axis=0, tiled=True)  77.7 us
    another operation x2, other arithmetic  18 us
    all_to_all x1, waiting for transfers between devices, body(): lax.all_to_all(key_send, 'seq', split_axis=1, concat_axis=0, tiled=True)  16.4 us
    slice x9, local copies, waits for them, and re-layouts, heads_attend(): heads_q[begin:finish]  15.5 us
    all_to_all x1, waiting for transfers between devices, body(): lax.all_to_all(value_send, 'seq', split_axis=1, concat_axis=0, tiled=True)  15.1 us
    gather x1, local copies, waits for them, and re-layouts, body(): returned.reshape(-1, width)[slot_index].reshape(local_tokens, TOPK, width)  12.4 us
  transfers between devices with their start and end apart: 5, of which 5 were waited for; matrix products, arithmetic and copies ran while one was open for 7% of the time, Pallas kernels for 0%

commit v1 on v0

v1 whole, which is shorter than its diff:
```python
import functools

import jax
import jax.numpy as jnp
from jax import lax
from jax.experimental import pallas as pl
from jax.experimental.pallas import tpu as pltpu
from jax.sharding import PartitionSpec as P

HEADS = 32
KV_HEADS = 4
HEAD_DIM = 128
TOPK = 8
SIDE = 4
CHIPS = SIDE * SIDE
CORES = 2
OFFSETS = (0, -1, 1, 2)
TOLD_ROWS = 32
LOG2E = 1.4426950408889634
ANY = pl.BlockSpec(memory_space=pl.ANY)
VMEM_LIMIT = 60 * 1024 * 1024


def pairs_of(dy, dx, swap):
    pairs = []
    for y in range(SIDE):
        for x in range(SIDE):
            for c in range(CORES):
                source = (y * SIDE + x) * CORES + c
                target = ((y + dy) % SIDE * SIDE + (x + dx) % SIDE) * CORES + (c ^ swap)
                pairs.append((source, target))
    return pairs


def along(value, axis, step):
    dy, dx = (step, 0) if axis == "y" else (0, step)
    return lax.ppermute(value, "seq", pairs_of(dy, dx, 0))


def to_sibling(value):
    return lax.ppermute(value, "seq", pairs_of(0, 0, 1))


def together(*values):
    return lax.optimization_barrier(values)


def near(a, b):
    a, b = together(a, b)
    got = [along(value, axis, step) for value, axis in ((a, "x"), (b, "y")) for step in (1, -1, 2)]
    got = together(*got)
    return together(
        jnp.concatenate([a, *got[:3]], axis=0), jnp.concatenate([b, *got[3:]], axis=0)
    )


def wide(a, b, beside):
    got = (along(a, "y", 1), along(a, "y", -1), along(b, "x", 1), along(b, "x", -1))
    return together(*got, *beside())


def wide_far(a, b, got, beside):
    ab, aa, bb, ba = got
    half_a, half_b = a.shape[0] // 2, b.shape[0] // 2
    far = (
        along(ab[:half_a], "y", 1),
        along(aa[half_a:], "y", -1),
        along(bb[:half_b], "x", 1),
        along(ba[half_b:], "x", -1),
    )
    a_low, a_high, b_low, b_high, *rest = together(*far, *beside())
    return [a, ab, aa, a_low, a_high, b, bb, ba, b_low, b_high], rest


def nothing():
    return ()


def locate(outer, inner, rows):
    if outer < 3:
        return outer, inner * rows
    return 3 + inner // 2, (inner % 2) * rows


def locate_out(outer, inner, rows):
    return 2 * outer + inner // 2, (inner % 2) * rows


def add(*terms):
    return functools.reduce(jnp.add, [term.astype(jnp.float32) for term in terms])


def scatter_both(partial):
    rounded = jnp.bfloat16
    sides = [(partial[:8], "y", "x"), (partial[8:], "x", "y")]
    far = []
    for parts, axis, _ in sides:
        far += [along(parts[6], axis, 1), along(parts[7], axis, -1)]
    *far, a3, a4, b3, b4 = together(*far, *(sides[i][0][j] for i in (0, 1) for j in (5, 2)))
    early = []
    for at, (high, low) in enumerate(((a3, a4), (b3, b4))):
        axis = sides[at][1]
        early += [along(high, axis, 1), along(low, axis, -1)]
    sends = []
    for at, (parts, _, _) in enumerate(sides):
        sends += [
            add(parts[4], far[2 * at]).astype(rounded),
            add(parts[3], far[2 * at + 1]).astype(rounded),
        ]
    *early, s0, s1, s2, s3 = together(*early, *sends)
    sends = (s0, s1, s2, s3)
    late = []
    for at, (_, axis, _) in enumerate(sides):
        late += [along(sends[2 * at], axis, 1), along(sends[2 * at + 1], axis, -1)]
    late = together(*late)
    inner = []
    for at, (parts, _, _) in enumerate(sides):
        low = add(parts[0], late[2 * at], early[2 * at + 1]).astype(rounded)
        high = add(parts[1], early[2 * at], late[2 * at + 1]).astype(rounded)
        rows = low.shape[0] // 2
        inner.append((low[:rows], low[rows:], high[:rows], high[rows:]))
    flat = together(*inner[0], *inner[1])
    got = []
    for at, (_, _, axis) in enumerate(sides):
        got += [along(flat[4 * at + 1 + i], axis, step) for i, step in enumerate((-1, 1, 2))]
    got = together(*got)
    return [add(flat[4 * at], *got[3 * at : 3 * at + 3]) for at in range(2)]


def attend_kernel(inner_first, info, q_ref, *refs):
    pieces, out_ref, k_scr, v_scr, sems = refs[:5], refs[5], refs[6], refs[7], refs[8]
    y, x = info[0], info[1]
    chip = y * SIDE + x
    block = 256

    def copies():
        made = []
        for outer in range(SIDE):
            for inner in range(SIDE):
                piece, row = locate(outer, inner, block + TOLD_ROWS if inner_first == "x" else block)
                ry, rx = (OFFSETS[outer], OFFSETS[inner])
                if inner_first == "y":
                    ry, rx = rx, ry
                home = lax.rem(y + ry + SIDE, SIDE) * SIDE + lax.rem(x + rx + SIDE, SIDE)
                home = pl.multiple_of(home * block, block)
                number = outer * SIDE + inner
                source = pieces[piece].at[pl.ds(row, block)]
                made.append(
                    pltpu.make_async_copy(
                        source.at[:, pl.ds(0, HEAD_DIM)],
                        k_scr.at[pl.ds(home, block)],
                        sems.at[0, number],
                    )
                )
                made.append(
                    pltpu.make_async_copy(
                        source.at[:, pl.ds(HEAD_DIM, HEAD_DIM)],
                        v_scr.at[pl.ds(home, block)],
                        sems.at[1, number],
                    )
                )
        return made

    @pl.when(pl.program_id(0) == 0)
    def _():
        for copy in copies():
            copy.start()
        for copy in copies():
            copy.wait()

    scale = HEAD_DIM ** (-0.5) * LOG2E
    keys = 2 * block
    q = jnp.concatenate([q_ref[:, :HEAD_DIM], q_ref[:, HEAD_DIM:]], axis=0)
    rows = q.shape[0]

    def step(at, carry, masked):
        top, total, acc = carry
        begin = pl.multiple_of(at * keys, keys)
        k = k_scr[pl.ds(begin, keys), :]
        v = v_scr[pl.ds(begin, keys), :]
        s = (
            lax.dot_general(q, k, (((1,), (1,)), ((), ())), preferred_element_type=jnp.float32)
            * scale
        )
        if masked:
            row = lax.broadcasted_iota(jnp.int32, s.shape, 0) % block + chip * block
            col = lax.broadcasted_iota(jnp.int32, s.shape, 1) + begin
            s = jnp.where(col <= row, s, -1e30)
        new_top = jnp.maximum(top, jnp.max(s, axis=1, keepdims=True))
        p = jnp.exp2(s - new_top)
        shrink = jnp.exp2(top - new_top)
        total = total * shrink + jnp.sum(p, axis=1, keepdims=True)
        acc = acc * shrink + jnp.dot(
            p.astype(jnp.bfloat16), v, preferred_element_type=jnp.float32
        )
        return new_top, total, acc

    carry = (
        jnp.full((rows, 1), -1e30, jnp.float32),
        jnp.zeros((rows, 1), jnp.float32),
        jnp.zeros((rows, HEAD_DIM), jnp.float32),
    )
    full = chip // 2
    carry = lax.fori_loop(0, full, functools.partial(step, masked=False), carry)
    _, total, acc = step(full, carry, True)
    out = (acc / total).astype(jnp.bfloat16)
    out_ref[:, :HEAD_DIM] = out[:block]
    out_ref[:, HEAD_DIM:] = out[block:]


def attend(info, q, pieces, inner_first):
    tokens, width = q.shape
    at_once = 2 * HEAD_DIM
    spec = pl.BlockSpec((tokens, at_once), lambda i, info: (0, i))
    keys = CHIPS * tokens
    return pl.pallas_call(
        functools.partial(attend_kernel, inner_first),
        out_shape=jax.ShapeDtypeStruct((tokens, width), jnp.bfloat16),
        grid_spec=pltpu.PrefetchScalarGridSpec(
            num_scalar_prefetch=1,
            grid=(width // at_once,),
            in_specs=[spec] + [ANY] * 5,
            out_specs=spec,
            scratch_shapes=[
                pltpu.VMEM((keys, HEAD_DIM), jnp.bfloat16),
                pltpu.VMEM((keys, HEAD_DIM), jnp.bfloat16),
                pltpu.SemaphoreType.DMA((2, CHIPS)),
            ],
        ),
        compiler_params=pltpu.CompilerParams(vmem_limit_bytes=VMEM_LIMIT),
        cost_estimate=pl.CostEstimate(
            flops=4 * tokens * width * keys, bytes_accessed=6 << 20, transcendentals=tokens * width * keys // 128
        ),
    )(info, q, *pieces)


def project_kernel(info, *refs):
    parts, w_ref, keep_ref, send_ref, w_scr, sems = refs[:-5], *refs[-5:]
    c = info[2]
    depth, width = parts[0].shape[1], w_ref.shape[1]
    tokens = keep_ref.shape[0]

    def copy_of(i):
        source = w_ref.at[pl.ds(pl.multiple_of((c * len(parts) + i) * depth, depth), depth)]
        return pltpu.make_async_copy(source, w_scr.at[i], sems.at[i])

    for i in range(len(parts)):
        copy_of(i).start()
    own = pl.ds(pl.multiple_of(c * tokens, tokens), tokens)
    other = pl.ds(pl.multiple_of((1 - c) * tokens, tokens), tokens)
    tile = 512
    for i in range(len(parts)):
        copy_of(i).wait()
    for rows, target in ((other, send_ref), (own, keep_ref)):
        for at in range(0, width, tile):
            product = sum(
                jnp.dot(
                    part[rows, :], w_scr[i, :, at : at + tile], preferred_element_type=jnp.float32
                )
                for i, part in enumerate(parts)
            )
            target[:, at : at + tile] = product.astype(target.dtype)


def project(info, parts, weight):
    width = weight.shape[1]
    tokens = parts[0].shape[0] // CORES
    vmem = pl.BlockSpec(memory_space=pltpu.VMEM)
    depth = parts[0].shape[1]
    return pl.pallas_call(
        project_kernel,
        out_shape=(
            jax.ShapeDtypeStruct((tokens, width), jnp.float32),
            jax.ShapeDtypeStruct((tokens, width), jnp.bfloat16),
        ),
        in_specs=[pl.BlockSpec(memory_space=pltpu.SMEM)] + [vmem] * len(parts) + [ANY],
        out_specs=(vmem, vmem),
        scratch_shapes=[
            pltpu.VMEM((len(parts), depth, width), jnp.bfloat16),
            pltpu.SemaphoreType.DMA((len(parts),)),
        ],
        compiler_params=pltpu.CompilerParams(vmem_limit_bytes=VMEM_LIMIT),
        cost_estimate=pl.CostEstimate(
            flops=4 * tokens * width * depth * len(parts), bytes_accessed=12 << 20, transcendentals=0
        ),
    )(info, *parts, weight)


def expert_kernel(
    row_ref,
    share_ref,
    gate_own,
    up_own,
    down_own,
    gate_sib,
    up_sib,
    down_sib,
    *refs,
):
    pieces, outs = refs[:10], refs[10:26]
    x_scr, h_scr, acc, y_scr, pick_scr, share_scr, in_sems, out_sems = refs[26:]
    expert, chunk = pl.program_id(0), pl.program_id(1)
    pair_count, pair_rows, pair_tokens = pick_scr.shape
    experts = 4
    slots = pair_rows // experts
    block = pair_tokens // 2
    width = x_scr.shape[2]
    half = width // 2

    def moves(hbm, out):
        made = []
        for side in range(2):
            for outer in range(SIDE):
                for inner in range(SIDE):
                    piece, row = (locate_out if out else locate)(outer, inner, block)
                    yi, xi = (outer, inner) if side == 0 else (inner, outer)
                    there = hbm[(8 if out else 5) * side + piece].at[pl.ds(row, block)]
                    here = x_scr.at[
                        yi * 2 + xi // 2, pl.ds((xi % 2) * block, block), pl.ds(side * half, half)
                    ]
                    sems = out_sems if out else in_sems
                    sem = sems.at[side, outer * SIDE + inner]
                    ends = (here, there) if out else (there, here)
                    made.append(pltpu.make_async_copy(*ends, sem))
        return made

    @pl.when((expert == 0) & (chunk == 0))
    def _():
        for copy in moves(pieces, False):
            copy.start()

        @pl.loop(0, pair_count)
        def _(pair):
            slot = lax.broadcasted_iota(jnp.int32, (pair_rows, pair_tokens), 0)
            pick = jnp.zeros((pair_rows, pair_tokens), jnp.float32)
            share = jnp.zeros((pair_rows, pair_tokens), jnp.float32)
            for r in range(TOPK):
                match = row_ref[pair, r : r + 1, :] == slot
                pick = jnp.where(match, 1.0, pick)
                share = jnp.where(match, share_ref[pair, r : r + 1, :], share)
            pick_scr[pair] = pick.astype(jnp.bfloat16)
            share_scr[pair] = jnp.sum(share, axis=1, keepdims=True)

        for copy in moves(pieces, False):
            copy.wait()

        @pl.loop(0, pair_count)
        def _(pair):
            for part in range(2):
                columns = pl.ds(part * half, half)
                rows = jnp.dot(
                    pick_scr[pair], x_scr[pair, :, columns], preferred_element_type=jnp.float32
                ).astype(jnp.bfloat16)
                for e in range(experts):
                    h_scr[e, pl.ds(pl.multiple_of(pair * slots, slots), slots), columns] = rows[
                        e * slots : (e + 1) * slots
                    ]

    def run(gate_ref, up_ref, down_ref):
        rows = h_scr[expert]
        gate = jnp.dot(rows, gate_ref[0], preferred_element_type=jnp.float32)
        up = jnp.dot(rows, up_ref[0], preferred_element_type=jnp.float32)
        hidden = (gate / (1.0 + jnp.exp(-gate)) * up).astype(jnp.bfloat16)
        for part in range(2):
            columns = pl.ds(part * half, half)
            product = jnp.dot(hidden, down_ref[0, :, columns], preferred_element_type=jnp.float32)

            @pl.when(chunk == 0)
            def _():
                acc[:, columns] = product

            @pl.when(chunk > 0)
            def _():
                acc[:, columns] += product

    @pl.when(expert < 2)
    def _():
        run(gate_own, up_own, down_own)

    @pl.when(expert >= 2)
    def _():
        run(gate_sib, up_sib, down_sib)

    last_chunk = chunk == pl.num_programs(1) - 1

    @pl.when(last_chunk)
    def _():
        for pair in range(pair_count):
            rows = acc[pair * slots : (pair + 1) * slots, :] * share_scr[
                pair, pl.ds(pl.multiple_of(expert * slots, slots), slots), :
            ]
            y_scr[pair, pl.ds(pl.multiple_of(expert * slots, slots), slots), :] = rows.astype(
                jnp.bfloat16
            )

    @pl.when(last_chunk & (expert == experts - 1))
    def _():
        @pl.loop(0, pair_count)
        def _(pair):
            for part in range(2):
                columns = pl.ds(part * half, half)
                x_scr[pair, :, columns] = lax.dot_general(
                    pick_scr[pair],
                    y_scr[pair, :, columns],
                    (((0,), (0,)), ((), ())),
                    preferred_element_type=jnp.float32,
                ).astype(jnp.bfloat16)

        for copy in moves(outs, True):
            copy.start()
        for copy in moves(outs, True):
            copy.wait()


def run_experts(row, share, own, sib, pieces):
    pair_count, _, pair_tokens = row.shape
    pair_rows = 4 * 2 * 3 * (pair_tokens // 2) * TOPK // (2 * 4 * CHIPS)
    width = own[0].shape[1]
    hidden = own[0].shape[2]
    chunks = 3
    tile = hidden // chunks
    experts = 4
    slots = pair_rows // experts
    whole = pl.BlockSpec(memory_space=pltpu.VMEM)

    def own_in(e, f):
        return (jnp.minimum(e, 1), 0, jnp.where(e < 2, f, chunks - 1))

    def own_out(e, f):
        return (jnp.minimum(e, 1), jnp.where(e < 2, f, chunks - 1), 0)

    def sib_in(e, f):
        return (jnp.maximum(e - 2, 0), 0, jnp.where(e < 2, 0, f))

    def sib_out(e, f):
        return (jnp.maximum(e - 2, 0), jnp.where(e < 2, 0, f), 0)

    rows = experts * pair_count * slots
    return pl.pallas_call(
        expert_kernel,
        grid=(experts, chunks),
        out_shape=[jax.ShapeDtypeStruct(pieces[3].shape, jnp.bfloat16)] * 16,
        in_specs=[
            whole,
            whole,
            pl.BlockSpec((1, width, tile), own_in),
            pl.BlockSpec((1, width, tile), own_in),
            pl.BlockSpec((1, tile, width), own_out),
            pl.BlockSpec((1, width, tile), sib_in),
            pl.BlockSpec((1, width, tile), sib_in),
            pl.BlockSpec((1, tile, width), sib_out),
        ]
        + [ANY] * 10,
        out_specs=[ANY] * 16,
        scratch_shapes=[
            pltpu.VMEM((pair_count, pair_tokens, width), jnp.bfloat16),
            pltpu.VMEM((experts, pair_count * slots, width), jnp.bfloat16),
            pltpu.VMEM((pair_count * slots, width), jnp.float32),
            pltpu.VMEM((pair_count, pair_rows, width), jnp.bfloat16),
            pltpu.VMEM((pair_count, pair_rows, pair_tokens), jnp.bfloat16),
            pltpu.VMEM((pair_count, pair_rows, 1), jnp.float32),
            pltpu.SemaphoreType.DMA((2, CHIPS)),
            pltpu.SemaphoreType.DMA((2, CHIPS)),
        ],
        compiler_params=pltpu.CompilerParams(vmem_limit_bytes=VMEM_LIMIT),
        cost_estimate=pl.CostEstimate(
            flops=6 * rows * width * hidden, bytes_accessed=56 << 20, transcendentals=rows * hidden
        ),
    )(row, share, *own, *sib, *pieces)


def told_routes(routes, route_gates, experts_all):
    tokens = routes.shape[0]
    share = route_gates / jnp.sum(route_gates, axis=1, keepdims=True)
    named = (routes[:, :, None] == jnp.arange(experts_all, dtype=jnp.int32)).astype(jnp.float32)
    hits = jnp.sum(named, axis=1)
    order = jnp.arange(tokens)
    earlier = (order[None, :] < order[:, None]).astype(jnp.bfloat16)
    rank = jnp.dot(earlier, hits.astype(jnp.bfloat16), preferred_element_type=jnp.float32)
    rank = jnp.sum(named * rank[:, None, :], axis=2)
    high = share.astype(jnp.bfloat16)
    left = share - high.astype(jnp.float32)
    mid = left.astype(jnp.bfloat16)
    low = (left - mid.astype(jnp.float32)).astype(jnp.bfloat16)
    first = jnp.concatenate([routes.astype(jnp.bfloat16).T, high.T, low.T], axis=0)
    second = jnp.concatenate([rank.astype(jnp.bfloat16).T, mid.T, jnp.zeros_like(low.T)], axis=0)
    told = jnp.concatenate([first, second], axis=1)
    return jnp.pad(told, ((0, TOLD_ROWS - 3 * TOPK), (0, 0)))


def route_tables(told, y, x, c):
    tokens = told.shape[2] // 2
    capacity = 3 * tokens * TOPK // (2 * 4 * CHIPS)
    expert = told[:, :TOPK, :tokens].astype(jnp.int32)
    rank = told[:, :TOPK, tokens:].astype(jnp.int32)
    share = (
        told[:, TOPK : 2 * TOPK, :tokens].astype(jnp.float32)
        + told[:, TOPK : 2 * TOPK, tokens:].astype(jnp.float32)
        + told[:, 2 * TOPK : 3 * TOPK, :tokens].astype(jnp.float32)
    )
    local = expert - (y * SIDE + x) * 4
    here = (local >= 0) & (local < 4)
    local = (local + 4 - 2 * c) % 4
    second = (jnp.arange(CHIPS, dtype=jnp.int32) % 2)[:, None, None]
    row = jnp.where(here, (local * 2 + second) * capacity + rank, -1)

    def paired(array):
        array = array.reshape(CHIPS // 2, 2, TOPK, tokens)
        return jnp.concatenate([array[:, 0], array[:, 1]], axis=2)

    return paired(row), paired(share)


def in_order(c, mine, theirs):
    return jnp.where(
        c == 0, jnp.concatenate([mine, theirs], axis=0), jnp.concatenate([theirs, mine], axis=0)
    )


def body(
    queries,
    key_vectors,
    value_vectors,
    residual,
    out_weight,
    norm_gain,
    routes,
    route_gates,
    w_gate,
    w_up,
    w_down,
):
    me = lax.axis_index("seq")
    c = me % CORES
    x = me // CORES % SIDE
    y = me // (CORES * SIDE)
    info = jnp.stack([y, x, c]).astype(jnp.int32)
    tokens, width = residual.shape
    experts_all = w_gate.shape[0] * lax.axis_size("seq")

    kv_half = key_vectors.shape[1] // 2
    q_half = queries.shape[1] // 2

    def half_of(array, which, size):
        return lax.dynamic_slice_in_dim(array, which * size, size, axis=1)

    def kv_of(which):
        k, v = (half_of(a, which, kv_half) for a in (key_vectors, value_vectors))
        d = HEAD_DIM
        return jnp.concatenate([k[:, :d], v[:, :d], k[:, d:], v[:, d:]], axis=1)

    kv_send, q_send = together(kv_of(1 - c), half_of(queries, 1 - c, q_half))
    kv = in_order(c, kv_of(c), to_sibling(kv_send))
    q_got = to_sibling(q_send)
    told = told_routes(routes, route_gates, experts_all)
    kv_a = jnp.concatenate([kv[:, : 2 * HEAD_DIM], told], axis=0)
    kv_b = kv[:, 2 * HEAD_DIM :]

    weight = lax.all_gather(out_weight, "seq", axis=0, tiled=True)
    own = (w_gate, w_up, w_down)

    kv_lines = near(kv_a, kv_b)
    kv_wide = wide(*kv_lines, nothing)
    kv_pieces, _ = wide_far(*kv_lines, kv_wide, nothing)
    q = in_order(c, half_of(queries, c, q_half), q_got)
    *sends, q = together(*own, q, kv_pieces[0])[:4]
    sib = [to_sibling(w) for w in sends]
    att_0 = attend(info, q[:, : q_half // 2], kv_pieces[:5], "x")
    att_1 = attend(info, q[:, q_half // 2 :], kv_pieces[5:], "y")

    keep, send = project(info, (att_0, att_1), weight)
    attn_sum = keep + to_sibling(send).astype(jnp.float32)
    stream = (residual.astype(jnp.float32) + attn_sum).astype(jnp.bfloat16)
    stream_f = stream.astype(jnp.float32)
    normed = (
        stream_f
        * lax.rsqrt(jnp.mean(stream_f * stream_f, axis=1, keepdims=True) + 1e-06)
        * norm_gain
    ).astype(jnp.bfloat16)

    told_rows = 2 * tokens + TOLD_ROWS
    told = []
    for outer in range(SIDE):
        for inner in range(SIDE):
            piece, first_row = locate(outer, inner, told_rows)
            first_row += 2 * tokens
            told.append(kv_pieces[piece][first_row : first_row + TOLD_ROWS])
    row, share = route_tables(jnp.stack(told), y, x, c)

    x_lines = near(normed[:, : width // 2], normed[:, width // 2 :])
    x_wide = wide(*x_lines, nothing)
    x_pieces, _ = wide_far(*x_lines, x_wide, nothing)
    partial = run_experts(row, share, own, sib, x_pieces)
    expert_sum = jnp.concatenate(scatter_both(partial), axis=1)
    layer_out = (stream_f + expert_sum).astype(jnp.bfloat16)
    return (stream, layer_out)


def solution(mesh):
    in_specs = (
        P(("dp", "seq"), None),
        P(("dp", "seq"), None),
        P(("dp", "seq"), None),
        P(("dp", "seq"), None),
        P("seq", None),
        P(),
        P(("dp", "seq"), None),
        P(("dp", "seq"), None),
        P("seq", None, None),
        P("seq", None, None),
        P("seq", None, None),
    )
    out_specs = (P(("dp", "seq"), None), P(("dp", "seq"), None))
    return jax.shard_map(body, mesh=mesh, in_specs=in_specs, out_specs=out_specs, check_vma=False)
```

time: 484 us -> 361 us (0.75); the launches traced: 475 us -> 359 us
  blocking collectives: 79.2 us -> 0 us
  starting transfers between devices: 21.1 us -> 99.8 us
  Pallas kernels: 0 us -> 64.1 us
  matrix products: 57.3 us -> 0.14 us
  waiting for transfers between devices: 208 us -> 151 us
  local copies, waits for them, and re-layouts: 64 us -> 19.4 us
  other arithmetic: 31 us -> 9.8 us
    ppermute x0 -> x52, waiting for transfers between devices: none -> 141 us  [the longest x46 139 us: along(): return lax.ppermute(value, 'seq', pairs_of(dy, dx, 0))]
    all_to_all x4 -> x0, waiting for transfers between devices: 113 us -> none  [the longest x1 77.7 us: body(): lax.all_to_all(expert_out, 'seq', split_axis=0, concat_axis=0, tiled=True)]
    ppermute x0 -> x52, starting transfers between devices: none -> 99.8 us  [the longest x46 98.6 us: along(): return lax.ppermute(value, 'seq', pairs_of(dy, dx, 0))]
    reduce_scatter x1 -> x0, waiting for transfers between devices: 94.1 us -> none  [body(): lax.psum_scatter(jnp.dot(attended, out_weight, preferred_element_type=jnp...]
    all_to_all x1 -> x0, blocking collectives: 79.2 us -> none  [body(): lax.all_to_all(send_rows, 'seq', split_axis=0, concat_axis=0, tiled=True)]
    pallas_call x0 -> x4, Pallas kernels: none -> 64.1 us  [the longest x1 41.7 us: run_experts(): pl.pallas_call(expert_kernel, grid=(experts, chunks), out_shape=[jax.Shap...]
    dot_general x21 -> x1, matrix products: 57.3 us -> 0.14 us  [told_routes(): jnp.dot(earlier, hits.astype(jnp.bfloat16), preferred_element_type=jnp.fl...]
    slice x25 -> x16, local copies, waits for them, and re-layouts: 26.7 us -> 5.33 us  [the longest x2 1.08 us: wide_far(): bb[:half_b]]
  transfers between devices with their start and end apart: 5 -> 53, of which waited for: 5 -> 32; matrix products, arithmetic and copies ran while one was open for 7% -> 7% of each run, Pallas kernels for 0% -> 4%
where the time goes in v1:
time: 361 us; the launch traced here: 359 us
  waiting for transfers between devices  151 us (42%)
  starting transfers between devices  99.8 us (28%)
  Pallas kernels  64.1 us (18%)
  local copies, waits for them, and re-layouts  19.4 us (5%)
  between operations  14.8 us (4%)
  other arithmetic  9.8 us (3%)
    ppermute x46, waiting for transfers between devices, along(): return lax.ppermute(value, 'seq', pairs_of(dy, dx, 0))  139 us
    ppermute x46, starting transfers between devices, along(): return lax.ppermute(value, 'seq', pairs_of(dy, dx, 0))  98.6 us
    pallas_call x1, Pallas kernels, run_experts(): pl.pallas_call(expert_kernel, grid=(experts, chunks), out_shape=[jax.Shap...  41.7 us
    pallas_call x2, Pallas kernels, attend(): pl.pallas_call(functools.partial(attend_kernel, inner_first), out_shape=j...  14.4 us
    unnamed x73, local copies, waits for them, and re-layouts  13.2 us
    all_gather x1, waiting for transfers between devices, body(): weight = lax.all_gather(out_weight, 'seq', axis=0, tiled=True)  9.02 us
    pallas_call x1, Pallas kernels, project(): pl.pallas_call(project_kernel, out_shape=(jax.ShapeDtypeStruct((tokens, w...  8.01 us
  transfers between devices with their start and end apart: 53, of which 32 were waited for; matrix products, arithmetic and copies ran while one was open for 7% of the time, Pallas kernels for 4%

profile of v1, /device:TPU:0, one launch (start us, length us, event | category | flops | bytes accessed | tf_op | source)
XLA Modules:
  0.0 359.0 jit_solution(503996532901086825)
XLA Ops:
  10.5 3.4 collective-permute-start.7
  31.4 14.0 %collective-permute-done.11.refs_2_ = bf16[1024,256]{1,0:T(8,128)(2,1)} collective-permute-done((bf16[1024,256]{1,0:T(8,128)(2,1)S(1)}, bf16[1024,256]{1,0:T(8,128)(2,1)}, u32[]{:S(2)}, u32[]{:S(2)}) %collective-permute-start.11) | collective-permute-done | bytes 524320 | tf_op jit(solution)/shard_map/ppermute | solution.py:37
  57.4 10.5 %collective-permute-done.15.refs_4_ = bf16[512,256]{1,0:T(8,128)(2,1)S(1)} collective-permute-done((bf16[512,256]{1,0:T(8,128)(2,1)S(1)}, bf16[512,256]{1,0:T(8,128)(2,1)S(1)}, u32[]{:S(2)}, u32[]{:S(2)}) %collective-permute-start.15) | collective-permute-done | bytes 262176 | tf_op jit(solution)/shard_map/ppermute | solution.py:37
  68.0 3.6 %collective-permute-done.14.refs_3_ = bf16[512,256]{1,0:T(8,128)(2,1)S(1)} collective-permute-done((bf16[512,256]{1,0:T(8,128)(2,1)S(1)}, bf16[512,256]{1,0:T(8,128)(2,1)S(1)}, u32[]{:S(2)}, u32[]{:S(2)}) %collective-permute-start.14) | collective-permute-done | bytes 262176 | tf_op jit(solution)/shard_map/ppermute | solution.py:37
  72.5 7.3 %shard_map.122.refs_0_ = bf16[256,1024]{1,0:T(8,128)(2,1)} custom-call(s32[3]{0:T(128)} %pad_add_fusion.1.info, bf16[256,1024]{1,0:T(8,128)(2,1)} %get-tuple-element.193.q_ref, bf16[1152,256]{1,0:T(8,128)(2,1)} %copy-done.4, bf16[1152,256]{1,0:T(8,128)(2,1)} %collective-permute-done.8.refs_1_, bf16[1152,256]{1,0:T(8,128)(2,1)} %copy-done.17, ...), custom_call_target="tpu_custom_call" | custom-call | flops 4294967296 | bytes 6291456 | tf_op jit(solution)/shard_map/pallas_call | solution.py:216
  79.8 7.2 %shard_map.123.refs_1_ = bf16[256,1024]{1,0:T(8,128)(2,1)} custom-call(s32[3]{0:T(128)} %pad_add_fusion.1.info, bf16[256,1024]{1,0:T(8,128)(2,1)} %get-tuple-element.192.q_ref, bf16[1024,256]{1,0:T(8,128)(2,1)} %copy-done.7, bf16[1024,256]{1,0:T(8,128)(2,1)} %collective-permute-done.10.refs_1_, bf16[1024,256]{1,0:T(8,128)(2,1)} %collective-permute-done.11.refs_2_, ...), custom_call_target="tpu_custom_call" | custom-call | flops 4294967296 | bytes 6291456 | tf_op jit(solution)/shard_map/pallas_call | solution.py:216
  87.0 9.0 %all-gather.2.cloned.1.call-done.refs_2_ = bf16[4096,2048]{1,0:T(8,128)(2,1)} async-done(((bf16[128,2048]{1,0:T(8,128)(2,1)}), bf16[4096,2048]{1,0:T(8,128)(2,1)}) %all-gather.2.cloned.1.call-update) | async-done | bytes 16777232 | tf_op jit(solution)/shard_map/all_gather | solution.py:559
  96.0 8.0 %shard_map.124 = (f32[128,2048]{1,0:T(8,128)}, bf16[128,2048]{1,0:T(8,128)(2,1)}) custom-call(s32[3]{0:T(128)} %pad_add_fusion.1.info, bf16[256,1024]{1,0:T(8,128)(2,1)} %shard_map.122.refs_0_, bf16[256,1024]{1,0:T(8,128)(2,1)} %shard_map.123.refs_1_, bf16[4096,2048]{1,0:T(8,128)(2,1)} %all-gather.2.cloned.1.call-done.refs_2_), custom_call_target="tpu_custom_call" | custom-call | flops 2147483648 | bytes 12582912 | tf_op jit(solution)/shard_map/pallas_call | solution.py:270
  113.2 4.9 %collective-permute-done.22 = bf16[128,1024]{1,0:T(8,128)(2,1)S(1)} collective-permute-done((bf16[128,1024]{1,0:T(8,128)(2,1)S(1)}, bf16[128,1024]{1,0:T(8,128)(2,1)S(1)}, u32[]{:S(2)}, u32[]{:S(2)}) %collective-permute-start.22) | collective-permute-done | bytes 262176 | tf_op jit(solution)/shard_map/ppermute | solution.py:37
  119.8 3.6 collective-permute-done.21
  123.3 15.7 %collective-permute-start.25 = (bf16[128,1024]{1,0:T(8,128)(2,1)S(1)}, bf16[128,1024]{1,0:T(8,128)(2,1)S(1)}, u32[]{:S(2)}, u32[]{:S(2)}) collective-permute-start(bf16[128,1024]{1,0:T(8,128)(2,1)S(1)} %get-tuple-element.123), channel_id=1, source_target_pairs={{0,16},{1,17},{2,18},{3,19},{4,20},{5,21},{6,22},{7,23},{8,24},{9,... | collective-permute-start | bytes 786440 | tf_op jit(solution)/shard_map/ppermute | solution.py:37
  140.5 13.1 %collective-permute-start.24 = (bf16[128,1024]{1,0:T(8,128)(2,1)S(1)}, bf16[128,1024]{1,0:T(8,128)(2,1)S(1)}, u32[]{:S(2)}, u32[]{:S(2)}) collective-permute-start(bf16[128,1024]{1,0:T(8,128)(2,1)S(1)} %get-tuple-element.123), channel_id=1, source_target_pairs={{0,24},{1,25},{2,26},{3,27},{4,28},{5,29},{6,30},{7,31},{8,0},{9,1... | collective-permute-start | bytes 786440 | tf_op jit(solution)/shard_map/ppermute | solution.py:37
  153.5 5.2 %collective-permute-start.23 = (bf16[128,1024]{1,0:T(8,128)(2,1)S(1)}, bf16[128,1024]{1,0:T(8,128)(2,1)S(1)}, u32[]{:S(2)}, u32[]{:S(2)}) collective-permute-start(bf16[128,1024]{1,0:T(8,128)(2,1)S(1)} %get-tuple-element.123), channel_id=1, source_target_pairs={{0,8},{1,9},{2,10},{3,11},{4,12},{5,13},{6,14},{7,15},{8,16},{9,17... | collective-permute-start | bytes 786440 | tf_op jit(solution)/shard_map/ppermute | solution.py:37
  171.7 16.4 %collective-permute-done.27.refs_2_ = bf16[512,1024]{1,0:T(8,128)(2,1)S(1)} collective-permute-done((bf16[512,1024]{1,0:T(8,128)(2,1)S(1)}, bf16[512,1024]{1,0:T(8,128)(2,1)S(1)}, u32[]{:S(2)}, u32[]{:S(2)}) %collective-permute-start.27) | collective-permute-done | bytes 1048608 | tf_op jit(solution)/shard_map/ppermute | solution.py:37
  196.1 14.7 %collective-permute-done.29.refs_7_ = bf16[512,1024]{1,0:T(8,128)(2,1)S(1)} collective-permute-done((bf16[512,1024]{1,0:T(8,128)(2,1)S(1)}, bf16[512,1024]{1,0:T(8,128)(2,1)S(1)}, u32[]{:S(2)}, u32[]{:S(2)}) %collective-permute-start.29) | collective-permute-done | bytes 1048608 | tf_op jit(solution)/shard_map/ppermute | solution.py:37
  210.8 3.9 %collective-permute-done.28.refs_6_ = bf16[512,1024]{1,0:T(8,128)(2,1)S(1)} collective-permute-done((bf16[512,1024]{1,0:T(8,128)(2,1)S(1)}, bf16[512,1024]{1,0:T(8,128)(2,1)S(1)}, u32[]{:S(2)}, u32[]{:S(2)}) %collective-permute-start.28) | collective-permute-done | bytes 1048608 | tf_op jit(solution)/shard_map/ppermute | solution.py:37
  218.4 6.2 %collective-permute-done.33.refs_9_ = bf16[256,1024]{1,0:T(8,128)(2,1)S(1)} collective-permute-done((bf16[256,1024]{1,0:T(8,128)(2,1)S(1)}, bf16[256,1024]{1,0:T(8,128)(2,1)S(1)}, u32[]{:S(2)}, u32[]{:S(2)}) %collective-permute-start.33) | collective-permute-done | bytes 524320 | tf_op jit(solution)/shard_map/ppermute | solution.py:37
  228.7 5.9 %collective-permute-done.31.refs_4_ = bf16[256,1024]{1,0:T(8,128)(2,1)S(1)} collective-permute-done((bf16[256,1024]{1,0:T(8,128)(2,1)S(1)}, bf16[256,1024]{1,0:T(8,128)(2,1)S(1)}, u32[]{:S(2)}, u32[]{:S(2)}) %collective-permute-start.31) | collective-permute-done | bytes 524320 | tf_op jit(solution)/shard_map/ppermute | solution.py:37
  234.5 3.8 %collective-permute-done.30.refs_3_ = bf16[256,1024]{1,0:T(8,128)(2,1)S(1)} collective-permute-done((bf16[256,1024]{1,0:T(8,128)(2,1)S(1)}, bf16[256,1024]{1,0:T(8,128)(2,1)S(1)}, u32[]{:S(2)}, u32[]{:S(2)}) %collective-permute-start.30) | collective-permute-done | bytes 524320 | tf_op jit(solution)/shard_map/ppermute | solution.py:37
  239.1 41.7 %shard_map.125 = (bf16[256,1024]{1,0:T(8,128)(2,1)}, bf16[256,1024]{1,0:T(8,128)(2,1)}, bf16[256,1024]{1,0:T(8,128)(2,1)}, bf16[256,1024]{1,0:T(8,128)(2,1)}, bf...) custom-call(s32[8,8,256]{2,1,0:T(8,128)} %pad_add_fusion.row_ref, ...), custom_call_target="tpu_custom_call" | custom-call | flops 14495514624 | bytes 58720256 | tf_op jit(solution)/shard_map/pallas_call | solution.py:439
  284.2 3.2 collective-permute-start.37
  287.4 4.8 %collective-permute-done.34 = bf16[256,1024]{1,0:T(8,128)(2,1)S(1)} collective-permute-done((bf16[256,1024]{1,0:T(8,128)(2,1)}, bf16[256,1024]{1,0:T(8,128)(2,1)S(1)}, u32[]{:S(2)}, u32[]{:S(2)}) %collective-permute-start.34) | collective-permute-done | bytes 524320 | tf_op jit(solution)/shard_map/ppermute | solution.py:37
  292.2 3.8 %collective-permute-done.36 = bf16[256,1024]{1,0:T(8,128)(2,1)S(1)} collective-permute-done((bf16[256,1024]{1,0:T(8,128)(2,1)}, bf16[256,1024]{1,0:T(8,128)(2,1)S(1)}, u32[]{:S(2)}, u32[]{:S(2)}) %collective-permute-start.36) | collective-permute-done | bytes 524320 | tf_op jit(solution)/shard_map/ppermute | solution.py:37
  296.0 3.2 collective-permute-start.39
  299.2 3.5 collective-permute-start.41
  305.7 3.3 collective-permute-done.38
  309.1 4.1 %collective-permute-done.40 = bf16[256,1024]{1,0:T(8,128)(2,1)S(1)} collective-permute-done((bf16[256,1024]{1,0:T(8,128)(2,1)}, bf16[256,1024]{1,0:T(8,128)(2,1)S(1)}, u32[]{:S(2)}, u32[]{:S(2)}) %collective-permute-start.40) | collective-permute-done | bytes 524320 | tf_op jit(solution)/shard_map/ppermute | solution.py:37
  313.1 3.2 collective-permute-start.43
  319.9 3.6 %collective-permute-done.42 = bf16[256,1024]{1,0:T(8,128)(2,1)S(1)} collective-permute-done((bf16[256,1024]{1,0:T(8,128)(2,1)S(1)}, bf16[256,1024]{1,0:T(8,128)(2,1)S(1)}, u32[]{:S(2)}, u32[]{:S(2)}) %collective-permute-start.42) | collective-permute-done | bytes 524320 | tf_op jit(solution)/shard_map/ppermute | solution.py:37
  323.5 6.8 %collective-permute-done.44 = bf16[256,1024]{1,0:T(8,128)(2,1)S(1)} collective-permute-done((bf16[256,1024]{1,0:T(8,128)(2,1)S(1)}, bf16[256,1024]{1,0:T(8,128)(2,1)S(1)}, u32[]{:S(2)}, u32[]{:S(2)}) %collective-permute-start.44) | collective-permute-done | bytes 524320 | tf_op jit(solution)/shard_map/ppermute | solution.py:37
  334.2 3.8 %collective-permute-start.46 = (bf16[128,1024]{1,0:T(8,128)(2,1)S(1)}, bf16[128,1024]{1,0:T(8,128)(2,1)S(1)}, u32[]{:S(2)}, u32[]{:S(2)}) collective-permute-start(bf16[128,1024]{1,0:T(8,128)(2,1)S(1)} %get-tuple-element.177), channel_id=1, source_target_pairs={{0,6},{1,7},{2,0},{3,1},{4,2},{5,3},{6,4},{7,5},{8,14},{9,15},{10,... | collective-permute-start | bytes 786440 | tf_op jit(solution)/shard_map/ppermute | solution.py:37
  342.0 6.4 %collective-permute-done.47 = bf16[128,1024]{1,0:T(8,128)(2,1)S(1)} collective-permute-done((bf16[128,1024]{1,0:T(8,128)(2,1)S(1)}, bf16[128,1024]{1,0:T(8,128)(2,1)S(1)}, u32[]{:S(2)}, u32[]{:S(2)}) %collective-permute-start.47) | collective-permute-done | bytes 262176 | tf_op jit(solution)/shard_map/ppermute | solution.py:37
  (208 shorter events, 96.6 us)
Async XLA Ops:
  7.2 88.8 %all-gather.2.cloned.1.call-start = ((), (), s32[]{:S(2)}) async-start(), calls=%async_computation | async-start | bytes 17301504 | tf_op jit(solution)/shard_map/all_gather | solution.py:559
  13.9 12.3 %collective-permute-start.4 = (bf16[288,256]{1,0:T(8,128)(2,1)S(1)}, bf16[288,256]{1,0:T(8,128)(2,1)S(1)}, u32[]{:S(2)}, u32[]{:S(2)}) collective-permute-start(bf16[288,256]{1,0:T(8,128)(2,1)S(1)} %pad_maximum_fusion.4), channel_id=1, source_target_pairs={{0,4},{1,5},{2,6},{3,7},{4,0},{5,1},{6,2},{7,3},{8,12},{9,13},{10,... | collective-permute-start | bytes 442376 | tf_op jit(solution)/shard_map/ppermute | solution.py:37
  26.3 21.7 %collective-permute-start.9 = (bf16[1152,256]{1,0:T(8,128)(2,1)S(1)}, bf16[1152,256]{1,0:T(8,128)(2,1)S(1)}, u32[]{:S(2)}, u32[]{:S(2)}) collective-permute-start(bf16[1152,256]{1,0:T(8,128)(2,1)S(1)} %pad_maximum_fusion.2.refs_0_), channel_id=1, source_target_pairs={{0,24},{1,25},{2,26},{3,27},{4,28},{5,29},{6,30},{7,31},{8,0},{9,1... | collective-permute-start | bytes 1769480 | tf_op jit(solution)/shard_map/ppermute | solution.py:37
  26.4 21.8 %collective-permute-start.8 = (bf16[1152,256]{1,0:T(8,128)(2,1)S(1)}, bf16[1152,256]{1,0:T(8,128)(2,1)}, u32[]{:S(2)}, u32[]{:S(2)}) collective-permute-start(bf16[1152,256]{1,0:T(8,128)(2,1)S(1)} %pad_maximum_fusion.2.refs_0_), channel_id=1, source_target_pairs={{0,8},{1,9},{2,10},{3,11},{4,12},{5,13},{6,14},{7,15},{8,16},{9,17... | collective-permute-start | bytes 1769480 | tf_op jit(solution)/shard_map/ppermute | solution.py:37
  28.4 17.0 %collective-permute-start.11 = (bf16[1024,256]{1,0:T(8,128)(2,1)S(1)}, bf16[1024,256]{1,0:T(8,128)(2,1)}, u32[]{:S(2)}, u32[]{:S(2)}) collective-permute-start(bf16[1024,256]{1,0:T(8,128)(2,1)S(1)} %pad_maximum_fusion.3.refs_0_), channel_id=1, source_target_pairs={{0,6},{1,7},{2,0},{3,1},{4,2},{5,3},{6,4},{7,5},{8,14},{9,15},{10,... | collective-permute-start | bytes 1572872 | tf_op jit(solution)/shard_map/ppermute | solution.py:37
  30.8 17.3 %collective-permute-start.10 = (bf16[1024,256]{1,0:T(8,128)(2,1)S(1)}, bf16[1024,256]{1,0:T(8,128)(2,1)}, u32[]{:S(2)}, u32[]{:S(2)}) collective-permute-start(bf16[1024,256]{1,0:T(8,128)(2,1)S(1)} %pad_maximum_fusion.3.refs_0_), channel_id=1, source_target_pairs={{0,2},{1,3},{2,4},{3,5},{4,6},{5,7},{6,0},{7,1},{8,10},{9,11},{10,... | collective-permute-start | bytes 1572872 | tf_op jit(solution)/shard_map/ppermute | solution.py:37
  30.8 20.6 %collective-permute-start = (bf16[128,2048]{1,0:T(8,128)(2,1)S(1)}, bf16[128,2048]{1,0:T(8,128)(2,1)S(1)}, u32[]{:S(2)}, u32[]{:S(2)}) collective-permute-start(bf16[128,2048]{1,0:T(8,128)(2,1)S(1)} %get-tuple-element.96), channel_id=1, source_target_pairs={{0,1},{1,0},{2,3},{3,2},{4,5},{5,4},{6,7},{7,6},{8,9},{9,8},{10,11... | collective-permute-start | bytes 1572872 | tf_op jit(solution)/shard_map/ppermute | solution.py:41
  49.3 22.3 %collective-permute-start.13 = (bf16[576,256]{1,0:T(8,128)(2,1)S(1)}, bf16[576,256]{1,0:T(8,128)(2,1)S(1)}, u32[]{:S(2)}, u32[]{:S(2)}) collective-permute-start(bf16[576,256]{1,0:T(8,128)(2,1)S(1)} %slice.177), channel_id=1, source_target_pairs={{0,24},{1,25},{2,26},{3,27},{4,28},{5,29},{6,30},{7,31},{8,0},{9,1... | collective-permute-start | bytes 884744 | tf_op jit(solution)/shard_map/ppermute | solution.py:37
  50.9 20.7 %collective-permute-start.12 = (bf16[576,256]{1,0:T(8,128)(2,1)S(1)}, bf16[576,256]{1,0:T(8,128)(2,1)S(1)}, u32[]{:S(2)}, u32[]{:S(2)}) collective-permute-start(bf16[576,256]{1,0:T(8,128)(2,1)S(1)} %slice.176), channel_id=1, source_target_pairs={{0,8},{1,9},{2,10},{3,11},{4,12},{5,13},{6,14},{7,15},{8,16},{9,17... | collective-permute-start | bytes 884744 | tf_op jit(solution)/shard_map/ppermute | solution.py:37
  53.7 14.3 %collective-permute-start.15 = (bf16[512,256]{1,0:T(8,128)(2,1)S(1)}, bf16[512,256]{1,0:T(8,128)(2,1)S(1)}, u32[]{:S(2)}, u32[]{:S(2)}) collective-permute-start(bf16[512,256]{1,0:T(8,128)(2,1)S(1)} %slice.179), channel_id=1, source_target_pairs={{0,6},{1,7},{2,0},{3,1},{4,2},{5,3},{6,4},{7,5},{8,14},{9,15},{10,... | collective-permute-start | bytes 786440 | tf_op jit(solution)/shard_map/ppermute | solution.py:37
  56.4 15.2 %collective-permute-start.14 = (bf16[512,256]{1,0:T(8,128)(2,1)S(1)}, bf16[512,256]{1,0:T(8,128)(2,1)S(1)}, u32[]{:S(2)}, u32[]{:S(2)}) collective-permute-start(bf16[512,256]{1,0:T(8,128)(2,1)S(1)} %slice.178), channel_id=1, source_target_pairs={{0,2},{1,3},{2,4},{3,5},{4,6},{5,7},{6,0},{7,1},{8,10},{9,11},{10,... | collective-permute-start | bytes 786440 | tf_op jit(solution)/shard_map/ppermute | solution.py:37
  104.4 134.0 %collective-permute-start.17 = (bf16[2,2048,768]{2,1,0:T(8,128)(2,1)}, bf16[2,2048,768]{2,1,0:T(8,128)(2,1)}, u32[]{:S(2)}, u32[]{:S(2)}) collective-permute-start(bf16[2,2048,768]{2,1,0:T(8,128)(2,1)} %gate_own.1), channel_id=1, source_target_pairs={{0,1},{1,0},{2,3},{3,2},{4,5},{5,4},{6,7},{7,6},{8,9},{9,8},{10,11... | collective-permute-start | bytes 18874376 | tf_op jit(solution)/shard_map/ppermute | solution.py:41
  104.6 133.7 %collective-permute-start.18 = (bf16[2,2048,768]{2,1,0:T(8,128)(2,1)}, bf16[2,2048,768]{2,1,0:T(8,128)(2,1)}, u32[]{:S(2)}, u32[]{:S(2)}) collective-permute-start(bf16[2,2048,768]{2,1,0:T(8,128)(2,1)} %up_own.1), channel_id=1, source_target_pairs={{0,1},{1,0},{2,3},{3,2},{4,5},{5,4},{6,7},{7,6},{8,9},{9,8},{10,11... | collective-permute-start | bytes 18874376 | tf_op jit(solution)/shard_map/ppermute | solution.py:41
  104.9 133.5 %collective-permute-start.19 = (bf16[2,768,2048]{2,1,0:T(8,128)(2,1)}, bf16[2,768,2048]{2,1,0:T(8,128)(2,1)}, u32[]{:S(2)}, u32[]{:S(2)}) collective-permute-start(bf16[2,768,2048]{2,1,0:T(8,128)(2,1)} %down_own.1), channel_id=1, source_target_pairs={{0,1},{1,0},{2,3},{3,2},{4,5},{5,4},{6,7},{7,6},{8,9},{9,8},{10,11... | collective-permute-start | bytes 18874376 | tf_op jit(solution)/shard_map/ppermute | solution.py:41
  110.6 12.8 %collective-permute-start.21 = (bf16[128,1024]{1,0:T(8,128)(2,1)S(1)}, bf16[128,1024]{1,0:T(8,128)(2,1)S(1)}, u32[]{:S(2)}, u32[]{:S(2)}) collective-permute-start(bf16[128,1024]{1,0:T(8,128)(2,1)S(1)} %get-tuple-element.122), channel_id=1, source_target_pairs={{0,6},{1,7},{2,0},{3,1},{4,2},{5,3},{6,4},{7,5},{8,14},{9,15},{10,... | collective-permute-start | bytes 786440 | tf_op jit(solution)/shard_map/ppermute | solution.py:37
  118.1 22.3 %collective-permute-start.20 = (bf16[128,1024]{1,0:T(8,128)(2,1)S(1)}, bf16[128,1024]{1,0:T(8,128)(2,1)S(1)}, u32[]{:S(2)}, u32[]{:S(2)}) collective-permute-start(bf16[128,1024]{1,0:T(8,128)(2,1)S(1)} %get-tuple-element.122), channel_id=1, source_target_pairs={{0,2},{1,3},{2,4},{3,5},{4,6},{5,7},{6,0},{7,1},{8,10},{9,11},{10,... | collective-permute-start | bytes 786440 | tf_op jit(solution)/shard_map/ppermute | solution.py:37
  123.3 30.2 %collective-permute-start.25 = (bf16[128,1024]{1,0:T(8,128)(2,1)S(1)}, bf16[128,1024]{1,0:T(8,128)(2,1)S(1)}, u32[]{:S(2)}, u32[]{:S(2)}) collective-permute-start(bf16[128,1024]{1,0:T(8,128)(2,1)S(1)} %get-tuple-element.123), channel_id=1, source_target_pairs={{0,16},{1,17},{2,18},{3,19},{4,20},{5,21},{6,22},{7,23},{8,24},{9,... | collective-permute-start | bytes 786440 | tf_op jit(solution)/shard_map/ppermute | solution.py:37
  140.5 22.2 %collective-permute-start.24 = (bf16[128,1024]{1,0:T(8,128)(2,1)S(1)}, bf16[128,1024]{1,0:T(8,128)(2,1)S(1)}, u32[]{:S(2)}, u32[]{:S(2)}) collective-permute-start(bf16[128,1024]{1,0:T(8,128)(2,1)S(1)} %get-tuple-element.123), channel_id=1, source_target_pairs={{0,24},{1,25},{2,26},{3,27},{4,28},{5,29},{6,30},{7,31},{8,0},{9,1... | collective-permute-start | bytes 786440 | tf_op jit(solution)/shard_map/ppermute | solution.py:37
  153.5 12.3 %collective-permute-start.23 = (bf16[128,1024]{1,0:T(8,128)(2,1)S(1)}, bf16[128,1024]{1,0:T(8,128)(2,1)S(1)}, u32[]{:S(2)}, u32[]{:S(2)}) collective-permute-start(bf16[128,1024]{1,0:T(8,128)(2,1)S(1)} %get-tuple-element.123), channel_id=1, source_target_pairs={{0,8},{1,9},{2,10},{3,11},{4,12},{5,13},{6,14},{7,15},{8,16},{9,17... | collective-permute-start | bytes 786440 | tf_op jit(solution)/shard_map/ppermute | solution.py:37
  166.0 22.1 %collective-permute-start.27 = (bf16[512,1024]{1,0:T(8,128)(2,1)S(1)}, bf16[512,1024]{1,0:T(8,128)(2,1)S(1)}, u32[]{:S(2)}, u32[]{:S(2)}) collective-permute-start(bf16[512,1024]{1,0:T(8,128)(2,1)S(1)} %pad_maximum_fusion.refs_0_), channel_id=1, source_target_pairs={{0,24},{1,25},{2,26},{3,27},{4,28},{5,29},{6,30},{7,31},{8,0},{9,1... | collective-permute-start | bytes 3145736 | tf_op jit(solution)/shard_map/ppermute | solution.py:37
  168.1 23.4 %collective-permute-start.26 = (bf16[512,1024]{1,0:T(8,128)(2,1)S(1)}, bf16[512,1024]{1,0:T(8,128)(2,1)S(1)}, u32[]{:S(2)}, u32[]{:S(2)}) collective-permute-start(bf16[512,1024]{1,0:T(8,128)(2,1)S(1)} %pad_maximum_fusion.refs_0_), channel_id=1, source_target_pairs={{0,8},{1,9},{2,10},{3,11},{4,12},{5,13},{6,14},{7,15},{8,16},{9,17... | collective-permute-start | bytes 3145736 | tf_op jit(solution)/shard_map/ppermute | solution.py:37
  188.1 22.7 %collective-permute-start.29 = (bf16[512,1024]{1,0:T(8,128)(2,1)S(1)}, bf16[512,1024]{1,0:T(8,128)(2,1)S(1)}, u32[]{:S(2)}, u32[]{:S(2)}) collective-permute-start(bf16[512,1024]{1,0:T(8,128)(2,1)S(1)} %pad_maximum_fusion.1.refs_5_), channel_id=1, source_target_pairs={{0,6},{1,7},{2,0},{3,1},{4,2},{5,3},{6,4},{7,5},{8,14},{9,15},{10,... | collective-permute-start | bytes 3145736 | tf_op jit(solution)/shard_map/ppermute | solution.py:37
  191.5 23.1 %collective-permute-start.28 = (bf16[512,1024]{1,0:T(8,128)(2,1)S(1)}, bf16[512,1024]{1,0:T(8,128)(2,1)S(1)}, u32[]{:S(2)}, u32[]{:S(2)}) collective-permute-start(bf16[512,1024]{1,0:T(8,128)(2,1)S(1)} %pad_maximum_fusion.1.refs_5_), channel_id=1, source_target_pairs={{0,2},{1,3},{2,4},{3,5},{4,6},{5,7},{6,0},{7,1},{8,10},{9,11},{10,... | collective-permute-start | bytes 3145736 | tf_op jit(solution)/shard_map/ppermute | solution.py:37
  280.9 11.3 %collective-permute-start.34 = (bf16[256,1024]{1,0:T(8,128)(2,1)}, bf16[256,1024]{1,0:T(8,128)(2,1)S(1)}, u32[]{:S(2)}, u32[]{:S(2)}) collective-permute-start(bf16[256,1024]{1,0:T(8,128)(2,1)} %get-tuple-element.141), channel_id=1, source_target_pairs={{0,8},{1,9},{2,10},{3,11},{4,12},{5,13},{6,14},{7,15},{8,16},{9,17... | collective-permute-start | bytes 1572872 | tf_op jit(solution)/shard_map/ppermute | solution.py:37
  284.2 11.8 %collective-permute-start.36 = (bf16[256,1024]{1,0:T(8,128)(2,1)}, bf16[256,1024]{1,0:T(8,128)(2,1)S(1)}, u32[]{:S(2)}, u32[]{:S(2)}) collective-permute-start(bf16[256,1024]{1,0:T(8,128)(2,1)} %get-tuple-element.143), channel_id=1, source_target_pairs={{0,2},{1,3},{2,4},{3,5},{4,6},{5,7},{6,0},{7,1},{8,10},{9,11},{10,... | collective-permute-start | bytes 1572872 | tf_op jit(solution)/shard_map/ppermute | solution.py:37
  284.2 11.8 %collective-permute-start.37 = (bf16[256,1024]{1,0:T(8,128)(2,1)}, bf16[256,1024]{1,0:T(8,128)(2,1)S(1)}, u32[]{:S(2)}, u32[]{:S(2)}) collective-permute-start(bf16[256,1024]{1,0:T(8,128)(2,1)} %get-tuple-element.144), channel_id=1, source_target_pairs={{0,6},{1,7},{2,0},{3,1},{4,2},{5,3},{6,4},{7,5},{8,14},{9,15},{10,... | collective-permute-start | bytes 1572872 | tf_op jit(solution)/shard_map/ppermute | solution.py:37
  296.0 13.1 %collective-permute-start.38 = (bf16[256,1024]{1,0:T(8,128)(2,1)}, bf16[256,1024]{1,0:T(8,128)(2,1)S(1)}, u32[]{:S(2)}, u32[]{:S(2)}) collective-permute-start(bf16[256,1024]{1,0:T(8,128)(2,1)} %get-tuple-element.149), channel_id=1, source_target_pairs={{0,8},{1,9},{2,10},{3,11},{4,12},{5,13},{6,14},{7,15},{8,16},{9,17... | collective-permute-start | bytes 1572872 | tf_op jit(solution)/shard_map/ppermute | solution.py:37
  296.0 13.1 %collective-permute-start.39 = (bf16[256,1024]{1,0:T(8,128)(2,1)}, bf16[256,1024]{1,0:T(8,128)(2,1)S(1)}, u32[]{:S(2)}, u32[]{:S(2)}) collective-permute-start(bf16[256,1024]{1,0:T(8,128)(2,1)} %get-tuple-element.150), channel_id=1, source_target_pairs={{0,24},{1,25},{2,26},{3,27},{4,28},{5,29},{6,30},{7,31},{8,0},{9,1... | collective-permute-start | bytes 1572872 | tf_op jit(solution)/shard_map/ppermute | solution.py:37
  299.2 13.9 %collective-permute-start.40 = (bf16[256,1024]{1,0:T(8,128)(2,1)}, bf16[256,1024]{1,0:T(8,128)(2,1)S(1)}, u32[]{:S(2)}, u32[]{:S(2)}) collective-permute-start(bf16[256,1024]{1,0:T(8,128)(2,1)} %get-tuple-element.151), channel_id=1, source_target_pairs={{0,2},{1,3},{2,4},{3,5},{4,6},{5,7},{6,0},{7,1},{8,10},{9,11},{10,... | collective-permute-start | bytes 1572872 | tf_op jit(solution)/shard_map/ppermute | solution.py:37
  299.2 13.9 %collective-permute-start.41 = (bf16[256,1024]{1,0:T(8,128)(2,1)}, bf16[256,1024]{1,0:T(8,128)(2,1)S(1)}, u32[]{:S(2)}, u32[]{:S(2)}) collective-permute-start(bf16[256,1024]{1,0:T(8,128)(2,1)} %get-tuple-element.152), channel_id=1, source_target_pairs={{0,6},{1,7},{2,0},{3,1},{4,2},{5,3},{6,4},{7,5},{8,14},{9,15},{10,... | collective-permute-start | bytes 1572872 | tf_op jit(solution)/shard_map/ppermute | solution.py:37
  316.4 13.9 %collective-permute-start.44 = (bf16[256,1024]{1,0:T(8,128)(2,1)S(1)}, bf16[256,1024]{1,0:T(8,128)(2,1)S(1)}, u32[]{:S(2)}, u32[]{:S(2)}) collective-permute-start(bf16[256,1024]{1,0:T(8,128)(2,1)S(1)} %add_convert_fusion.5), channel_id=1, source_target_pairs={{0,2},{1,3},{2,4},{3,5},{4,6},{5,7},{6,0},{7,1},{8,10},{9,11},{10,... | collective-permute-start | bytes 1572872 | tf_op jit(solution)/shard_map/ppermute | solution.py:37
  318.1 14.1 %collective-permute-start.45 = (bf16[256,1024]{1,0:T(8,128)(2,1)S(1)}, bf16[256,1024]{1,0:T(8,128)(2,1)S(1)}, u32[]{:S(2)}, u32[]{:S(2)}) collective-permute-start(bf16[256,1024]{1,0:T(8,128)(2,1)S(1)} %add_convert_fusion.4), channel_id=1, source_target_pairs={{0,6},{1,7},{2,0},{3,1},{4,2},{5,3},{6,4},{7,5},{8,14},{9,15},{10,... | collective-permute-start | bytes 1572872 | tf_op jit(solution)/shard_map/ppermute | solution.py:37
  (50 other events, 836.1 us)
Sparse Core Ops, SparseCore 0:
  10.3 85.6 all-gather.1
